TPU v7x, 32 devices: a whole 2x2x4 slice. The times are simulated.
32 devices in a mesh: groups: 2 (over x), tensor: 16 (over z, y, core).
Axes of the slice: x: 2, y: 2, z: 4, core: 2. Of those that a mesh axis runs over, the one named last changes fastest.
Arguments:
- resid: bfloat16 [128, 8192], P(('groups', 'tensor')), parts along dimension 0, may hold values from -6 to 6
- labels: int32 [128, 1], P(('groups', 'tensor')), parts along dimension 0, may hold values from 0 to 7
- erase_mean: float32 [8192], replicated, may hold values from -3 to 3
- erase_down: float32 [8192, 8], replicated, may hold values from -0.0625 to 0.0625
- erase_up: float32 [8, 8192], replicated, may hold values from -2 to 2
- norm_gain: float32 [8192], replicated, may hold values from 0.25 to 1.75
- w_gate: bfloat16 [8192, 14336], P(None, 'tensor'), may hold values from -0.0625 to 0.0625
- w_up: bfloat16 [8192, 14336], P(None, 'tensor'), may hold values from -0.0625 to 0.0625
- w_down: bfloat16 [14336, 8192], P('tensor'), may hold values from -0.046875 to 0.046875
Outputs:
- block_out: bfloat16 [128, 8192], P(('groups', 'tensor')), parts along dimension 0
- class_dev: float32 [16, 8192], P('groups', 'tensor'), parts along dimension 0
- covariance: bfloat16 [16384, 8192], P(('groups', 'tensor')), parts along dimension 0
There are 2 independent parts, one for each index of `groups`. A program takes and returns all parts, laid end to end along the dimension named above; an argument that names none is the same for every part. Nothing has to cross between parts.
Inputs may be any that keep to these rules, and one draw needn't show every extreme that they name: Every class 0 to 7 labels at least one row of a group.
All inputs are finite; a program needn't handle non-finite values.
Results may differ from a plain program's by a relative error of at most 0.013.
Values may be sent and summed in bfloat16 or wider, within the bound.
A program may use at most 128 MiB of HBM per device.

v0:
```python
import jax
import jax.numpy as jnp
from jax import lax
from jax.sharding import PartitionSpec as P

D = 8192
CLASSES = 8


def class_table(label_rows):
    return (label_rows[:, 0][:, None] == jnp.arange(CLASSES, dtype=jnp.int32)[None, :]).astype(
        jnp.float32
    )


def body(resid, labels, erase_mean, erase_down, erase_up, norm_gain, w_gate, w_up, w_down):
    highest = lax.Precision.HIGHEST
    ranks = lax.axis_size("tensor")
    own = lax.axis_index("tensor")
    total_rows = resid.shape[0] * ranks
    width = D // ranks
    x = resid.astype(jnp.float32)
    proj = jnp.dot(x - erase_mean, erase_down, precision=highest)
    scrubbed = (x - jnp.dot(proj, erase_up, precision=highest)).astype(jnp.bfloat16)
    xs = scrubbed.astype(jnp.float32)
    normed = (xs * lax.rsqrt(jnp.mean(xs * xs, axis=1, keepdims=True) + 1e-05) * norm_gain).astype(
        jnp.bfloat16
    )
    piece = lax.all_gather(normed, "tensor", axis=0, tiled=True)
    gate = jnp.dot(piece, w_gate, preferred_element_type=jnp.float32)
    up = jnp.dot(piece, w_up, preferred_element_type=jnp.float32)
    hidden = (jax.nn.silu(gate) * up).astype(jnp.bfloat16)
    summed = lax.psum_scatter(
        jnp.dot(hidden, w_down, preferred_element_type=jnp.float32),
        "tensor",
        scatter_dimension=0,
        tiled=True,
    )
    block_out = (xs + summed).astype(jnp.bfloat16)
    yf = block_out.astype(jnp.float32)
    onehot = class_table(labels)
    class_sums, counts = lax.psum(
        (jnp.dot(onehot.T, yf, precision=highest), jnp.sum(onehot, axis=0)), "tensor"
    )
    mean = jnp.sum(class_sums, axis=0) / total_rows
    deviation = class_sums / counts[:, None] - mean
    class_dev = lax.dynamic_slice_in_dim(deviation, own * width, width, 1)
    centred = (yf - mean).astype(jnp.bfloat16)
    piece = lax.all_gather(centred, "tensor", axis=0, tiled=True)
    owned = lax.dynamic_slice_in_dim(piece, own * width, width, 1)
    gram = lax.dot_general(
        owned, piece, (((0,), (0,)), ((), ())), preferred_element_type=jnp.float32
    )
    covariance = (gram / total_rows).astype(jnp.bfloat16)
    return (block_out, class_dev, covariance)


def solution(mesh):
    return jax.shard_map(
        body,
        mesh=mesh,
        in_specs=(
            P(("groups", "tensor"), None),
            P(("groups", "tensor"), None),
            P(),
            P(),
            P(),
            P(),
            P(None, "tensor"),
            P(None, "tensor"),
            P("tensor", None),
        ),
        out_specs=(
            P(("groups", "tensor"), None),
            P("groups", "tensor"),
            P(("groups", "tensor"), None),
        ),
        check_vma=False,
    )
```

profile of v0, /device:TPU:11, one launch (start us, length us, event | category | flops | bytes accessed | tf_op | source)
XLA Modules:
  0.0 319.6 jit_solution(13621881090041405473)
XLA Ops:
  7.2 0.0 copy-start
  7.2 0.0 all-gather.5.cloned.1.call-start
  7.2 1.7 fusion.9
  8.9 0.0 copy-done
  8.9 1.4 multiply_reduce_fusion
  10.3 1.5 fusion.12
  11.8 0.0 all-gather.5.cloned.1.call-update
  11.8 0.0 all-reduce.6.cloned.1.call-start
  11.8 38.6 %all-gather.5.cloned.1.call-done = bf16[16,4,8192]{2,1,0:T(4,128)(2,1)} async-done(((bf16[1,4,8192]{2,1,0:T(4,128)(2,1)}), bf16[16,4,8192]{2,1,0:T(4,128)(2,1)}) %all-gather.5.cloned.1.call-update) | async-done | bytes 1048592 | tf_op jit(solution)/shard_map/all_gather | solution.py:29
  50.5 1.3 reshape.21
  51.8 7.6 %fusion.21 = f32[64,896]{1,0:T(8,128)S(1)} fusion(bf16[64,8192]{1,0:T(8,128)(2,1)S(1)} %reshape.21, bf16[8192,896]{1,0:T(8,128)(2,1)} %param.15), kind=kOutput, calls=%fused_computation.34 | convolution fusion | flops 939524096 | bytes 15958016 | tf_op jit(solution)/shard_map/dot_general | solution.py:30
  59.4 0.0 copy-start.3
  59.4 0.0 copy-start.2
  59.4 16.0 %fusion.3 = f32[64,8192]{1,0:T(8,128)} fusion(bf16[896,8192]{1,0:T(8,128)(2,1)} %param.17, bf16[64,8192]{1,0:T(8,128)(2,1)S(1)} %reshape.21, bf16[8192,896]{1,0:T(8,128)(2,1)} %param.16, f32[64,896]{1,0:T(8,128)S(1)} %fusion.21), kind=kOutput, calls=%fused_computation.6 | convolution fusion | flops 1879392256 | bytes 32735232 | tf_op jit(solution)/shard_map/dot_general | solution.py:34
  75.4 0.0 all-reduce.6.cloned.1.call-update
  75.4 0.0 all-reduce.4.cloned.1.call-start
  75.4 0.0 copy-done.3
  75.5 0.6 dynamic-slice
  76.7 94.6 %all-reduce.6.cloned.1.call-done = f32[64,8192]{1,0:T(8,128)} async-done(((f32[64,8192]{1,0:T(8,128)}), f32[64,8192]{1,0:T(8,128)}) %all-reduce.6.cloned.1.call-update) | async-done | bytes 2097168
  171.3 1.0 fusion.10
  172.3 0.0 copy-start.1
  172.3 0.0 copy-done.2
  172.3 1.0 fusion.17
  173.3 0.0 all-reduce.4.cloned.1.call-update
  173.4 0.0 all-gather.7.cloned.1.call-start
  173.4 91.2 %all-reduce.4.cloned.1.call-done = f32[8,8192]{1,0:T(8,128)} async-done(((f32[8,8192]{1,0:T(8,128)}), f32[8,8192]{1,0:T(8,128)}) %all-reduce.4.cloned.1.call-update) | async-done | bytes 262160 | tf_op jit(solution)/shard_map/psum | solution.py:42
  264.6 1.0 reduce_sum.29
  265.7 0.7 fusion.13
  266.3 0.0 all-gather.7.cloned.1.call-update
  266.4 0.1 convert_reduce_fusion
  266.4 24.4 %psum.15 = f32[8]{0:T(128)S(1)} all-reduce(f32[8]{0:T(128)S(1)} %convert_reduce_fusion), channel_id=1, replica_groups=mesh['groups'=2,'tensor'=16] {'tensor'}, use_global_device_ids=true, to_apply=%region_4.5 | all-reduce | flops 8 | bytes 64 | tf_op jit(solution)/shard_map/psum | solution.py:42
  290.8 0.1 dynamic-slice.2
  290.9 1.4 fusion.16
  292.3 13.6 %all-gather.7.cloned.1.call-done = bf16[16,4,8192]{2,1,0:T(4,128)(2,1)} async-done(((bf16[1,4,8192]{2,1,0:T(4,128)(2,1)}), bf16[16,4,8192]{2,1,0:T(4,128)(2,1)}) %all-gather.7.cloned.1.call-update) | async-done | bytes 1048592 | tf_op jit(solution)/shard_map/all_gather | solution.py:49
  305.9 1.3 reshape.23
  307.2 5.8 %multiply_convert_fusion = bf16[512,8192]{1,0:T(8,128)(2,1)} fusion(bf16[64,8192]{1,0:T(8,128)(2,1)S(1)} %reshape.23, s32[]{:T(128)S(6)} %select_n.4), kind=kOutput, calls=%fused_computation | convolution fusion | flops 545259520 | bytes 9502724 | tf_op jit(solution)/shard_map/dot_general | solution.py:51
  313.0 0.0 copy-done.1
  (2 shorter events, 0.0 us)
Async XLA Ops:
  7.2 1.7 copy-start
  7.2 43.3 %all-gather.5.cloned.1.call-start = ((), (), s32[]{:S(2)}) async-start(), calls=%async_computation.1 | async-start | bytes 1114112 | tf_op jit(solution)/shard_map/all_gather | solution.py:29
  11.8 159.5 %all-reduce.6.cloned.1.call-start = ((), (), s32[]{:S(2)}) async-start(), calls=%async_computation.3 | async-start | bytes 4194304
  59.4 16.1 %copy-start.3 = (u32[32]{0:T(128)S(1)}, u32[32]{0:T(128)}, u32[]{:S(2)}) copy-start(u32[32]{0:T(128)} %constant.29) | copy-start | bytes 388
  59.4 112.9 %copy-start.2 = (s32[4,1]{0,1:T(1,128)S(1)}, s32[4,1]{0,1:T(1,128)}, u32[]{:S(2)}) copy-start(s32[4,1]{0,1:T(1,128)} %param.10) | copy-start | bytes 52
  75.4 189.2 %all-reduce.4.cloned.1.call-start = ((), (), s32[]{:S(2)}) async-start(), calls=%async_computation | async-start | bytes 524288 | tf_op jit(solution)/shard_map/psum | solution.py:42
  172.3 140.7 %copy-start.1 = (bf16[4,8192]{1,0:T(4,128)(2,1)}, bf16[4,8192]{1,0:T(4,128)(2,1)S(1)}, u32[]{:S(2)}) copy-start(bf16[4,8192]{1,0:T(4,128)(2,1)S(1)} %fusion.10) | copy-start | bytes 196612
  173.4 132.6 %all-gather.7.cloned.1.call-start = ((), (), s32[]{:S(2)}) async-start(), calls=%async_computation.2 | async-start | bytes 1114112 | tf_op jit(solution)/shard_map/all_gather | solution.py:49
Sparse Core Ops, SparseCore 0:
  11.9 38.5 all-gather.4
  75.5 95.7 all-reduce.5
  175.7 88.9 all-reduce.3
  267.5 38.3 all-gather.6
where the time goes:
time: 322 us; the launch traced here: 320 us
  waiting for transfers between devices  238 us (74%)
  matrix products  33.3 us (10%)
  blocking collectives  24.4 us (8%)
  between operations  14.5 us (5%)
  other arithmetic  5.66 us (2%)
  local copies, waits for them, and re-layouts  3.35 us (1%)
    unnamed x5, waiting for transfers between devices  94.7 us
    psum x1, waiting for transfers between devices, body(): lax.psum((jnp.dot(onehot.T, yf, precision=highest), jnp.sum(onehot, axis=...  91.2 us
    all_gather x1, waiting for transfers between devices, body(): piece = lax.all_gather(normed, 'tensor', axis=0, tiled=True)  38.6 us
    psum x1, blocking collectives, body(): lax.psum((jnp.dot(onehot.T, yf, precision=highest), jnp.sum(onehot, axis=...  24.4 us
    dot_general x1, matrix products, body(): jnp.dot(hidden, w_down, preferred_element_type=jnp.float32)  16 us
    all_gather x1, waiting for transfers between devices, body(): piece = lax.all_gather(centred, 'tensor', axis=0, tiled=True)  13.6 us
    dot_general x1, matrix products, body(): gate = jnp.dot(piece, w_gate, preferred_element_type=jnp.float32)  7.56 us
  transfers between devices with their start and end apart: 4, of which 4 were waited for; matrix products, arithmetic and copies ran while one was open for 1% of the time, Pallas kernels for 0%

commit v1 on v0

v1 whole, which is shorter than its diff:
```python
import functools

import jax
import jax.numpy as jnp
from jax import lax
from jax.experimental import pallas as pl
from jax.experimental.pallas import tpu as pltpu
from jax.sharding import PartitionSpec as P

CLASSES = 8
EPS = 1e-05
TILE = 16
LANES = 128
MIB = 1 << 20
Z, Y, C = 4, 2, 2


def place():
    me = lax.axis_index("tensor")
    return me, me // (Y * C), (me // C) % Y, me % C


def index_of(z, y, c):
    return (z * Y + y) * C + c


def at_rows(ref, block, rows):
    return ref.at[pl.ds(pl.multiple_of(block * rows, rows), rows)]


def remote(src, dst, send, recv, peer):
    return pltpu.make_async_remote_copy(
        src_ref=src,
        dst_ref=dst,
        send_sem=send,
        recv_sem=recv,
        device_id={"tensor": peer},
        device_id_type=pl.DeviceIdType.MESH,
    )


def all_gather(buf, rows, send, recv):
    me, z, y, c = place()
    sibling = index_of(z, y, 1 - c)
    across = index_of(z, 1 - y, c)
    started = []

    def push(block, peer):
        part = at_rows(buf, block, rows)
        copy = remote(part, part, send.at[len(started)], recv.at[block], peer)
        copy.start()
        started.append(copy)

    def await_block(block, peer):
        part = at_rows(buf, block, rows)
        remote(part, part, send.at[0], recv.at[block], peer).wait_recv()

    for dz in (2, 1, 3):
        push(me, index_of((z + dz) % Z, y, c))
    push(me, across)
    push(me, sibling)
    for dz in (1, 3, 2):
        block = index_of((z + dz) % Z, y, c)
        await_block(block, block)
        push(block, across)
        push(block, sibling)
    for dz in (0, 1, 3, 2):
        block = index_of((z + dz) % Z, 1 - y, c)
        await_block(block, across)
        push(block, sibling)
    for dz in (0, 1, 3, 2):
        for to in (y, 1 - y):
            await_block(index_of((z + dz) % Z, to, 1 - c), sibling)
    return started


def mlp_kernel(
    own_rows,
    block_ref,
    gain_ref,
    wg_hbm,
    wu_hbm,
    wd_hbm,
    y_hbm,
    lab_ref,
    xg,
    xs,
    xn,
    wg,
    wu,
    wd,
    gate,
    up,
    hidden,
    s_core,
    r_core,
    s_y,
    r_y,
    s_z,
    r_z,
    out,
    g_sem,
    u_sem,
    d_sem,
    ag1_send,
    ag1_recv,
    ag2_send,
    ag2_recv,
    core_send,
    core_recv,
    y_send,
    y_recv,
    z_send,
    z_recv,
    o_sem,
):
    n = Z * Y * C
    rows, depth = xs.shape
    width = depth // n
    quarters = TILE // own_rows
    cols = depth // quarters
    me, z, y, c = place()
    sibling = index_of(z, y, 1 - c)
    across = index_of(z, 1 - y, c)
    chunks = g_sem.shape[0]
    kc = depth // chunks

    def load_gate(k):
        part = pl.ds(pl.multiple_of(k * kc, kc), kc)
        return pltpu.make_async_copy(wg_hbm.at[part], wg.at[part], g_sem.at[k])

    def load_up(k):
        part = pl.ds(pl.multiple_of(k * kc, kc), kc)
        return pltpu.make_async_copy(wu_hbm.at[part], wu.at[part], u_sem.at[k])

    def load_down(pos, block):
        part = pl.ds(pl.multiple_of(block * width, width), width)
        return pltpu.make_async_copy(wd_hbm.at[:, part], wd.at[pos], d_sem.at[pos])

    order = (
        [index_of(k, 1 - y, 1 - c) for k in range(Z)]
        + [index_of(k, y, 1 - c) for k in range(Z)]
        + [index_of(k, 1 - y, c) for k in range(Z)]
        + [index_of((z + dz) % Z, y, c) for dz in (2, 1, 3)]
        + [me]
    )

    barrier = pltpu.get_barrier_semaphore()
    peers = [index_of((z + dz) % Z, y, c) for dz in (1, 2, 3)] + [across, sibling]
    for peer in peers:
        pl.semaphore_signal(
            barrier, inc=1, device_id={"tensor": peer}, device_id_type=pl.DeviceIdType.MESH
        )
    for k in range(chunks):
        load_gate(k).start()
        load_up(k).start()
    for pos in range(n):
        load_down(pos, order[pos]).start()
    own_part = pl.ds(pl.multiple_of(me * TILE, TILE), TILE)
    xg[own_part, :] = block_ref[...]
    pl.semaphore_wait(barrier, len(peers))

    started = all_gather(xg, TILE, ag1_send, ag1_recv)

    row = lax.broadcasted_iota(jnp.int32, (rows, n * TILE), 0)
    col = lax.broadcasted_iota(jnp.int32, (rows, n * TILE), 1)
    base = (row // own_rows) * TILE + row % own_rows
    picks = [
        jnp.where(col == base + q * own_rows, 1.0, 0.0).astype(jnp.bfloat16)
        for q in range(quarters)
    ]
    step = 512
    lab_ref[...] = jnp.dot(
        picks[0], xg[:, cols : cols + LANES], preferred_element_type=jnp.float32
    )

    def spread(i, total):
        at = pl.multiple_of(i * step, step)
        taken = xg[:, pl.ds(at, step)]
        for q in range(quarters):
            part = jnp.dot(picks[q], taken, preferred_element_type=jnp.float32)
            xs[:, pl.ds(pl.multiple_of(q * cols + at, step), step)] = part.astype(jnp.bfloat16)
            total = total + part * part
        return total

    total = lax.fori_loop(0, cols // step, spread, jnp.zeros((rows, step), jnp.float32))
    scale = lax.rsqrt(jnp.sum(total, axis=1, keepdims=True) / depth + EPS)

    def norm(i, carry):
        at = pl.ds(pl.multiple_of(i * step, step), step)
        xn[:, at] = (xs[:, at].astype(jnp.float32) * scale * gain_ref[:, at]).astype(jnp.bfloat16)
        return carry

    lax.fori_loop(0, depth // step, norm, 0)

    gate[...] = jnp.zeros_like(gate)
    up[...] = jnp.zeros_like(up)

    def project(k, carry):
        part = pl.ds(pl.multiple_of(k * kc, kc), kc)
        left = xn[:, part]
        load_gate(k).wait()
        gate[...] += jnp.dot(left, wg[part, :], preferred_element_type=jnp.float32)
        load_up(k).wait()
        up[...] += jnp.dot(left, wu[part, :], preferred_element_type=jnp.float32)
        return carry

    lax.fori_loop(0, chunks, project, 0)
    gated = gate[...]
    hidden[...] = (gated / (1.0 + jnp.exp(-gated)) * up[...]).astype(jnp.bfloat16)

    def share(pos, block):
        load_down(pos, block).wait()
        return jnp.dot(hidden[...], wd[pos], preferred_element_type=jnp.float32)

    def core_copy(k):
        return remote(s_core.at[k], r_core.at[k], core_send.at[k], core_recv.at[k], sibling)

    def y_copy(k):
        return remote(s_y.at[k], r_y.at[k], y_send.at[k], y_recv.at[k], across)

    def z_copy(dz):
        return remote(
            s_z.at[dz - 1],
            r_z.at[dz - 1],
            z_send.at[dz - 1],
            z_recv.at[dz - 1],
            index_of((z + dz) % Z, y, c),
        )

    def to_core(k, carry):
        block = index_of(k % Z, jnp.where(k < Z, 1 - y, y), 1 - c)
        s_core[k] = share(k, block).astype(jnp.bfloat16)
        core_copy(k).start()
        return carry

    lax.fori_loop(0, 2 * Z, to_core, 0)

    def to_y(k, carry):
        mine = share(2 * Z + k, index_of(k, 1 - y, c))
        core_copy(k).wait_recv()
        s_y[k] = (mine + r_core[k].astype(jnp.float32)).astype(jnp.bfloat16)
        y_copy(k).start()
        return carry

    lax.fori_loop(0, Z, to_y, 0)

    def chip_rows(pos, to):
        mine = share(pos, index_of(to, y, c))
        core_copy(Z + to).wait_recv()
        y_copy(to).wait_recv()
        return mine + r_core[Z + to].astype(jnp.float32) + r_y[to].astype(jnp.float32)

    for i, dz in enumerate((2, 1, 3)):
        s_z[dz - 1] = chip_rows(3 * Z + i, (z + dz) % Z).astype(jnp.bfloat16)
        z_copy(dz).start()
    summed = chip_rows(n - 1, z)
    for dz in (1, 3, 2):
        z_copy(dz).wait_recv()
        summed = summed + r_z[dz - 1].astype(jnp.float32)
    mine = pl.ds(pl.multiple_of(me * width, width), width)
    kept = (xs[:, mine].astype(jnp.float32) + summed).astype(jnp.bfloat16)
    out[pl.ds(pl.multiple_of(me * rows, rows), rows), :] = kept

    started += all_gather(out, rows, ag2_send, ag2_recv)
    store = pltpu.make_async_copy(out, y_hbm, o_sem)
    store.start()
    for copy in started:
        copy.wait_send()

    def finish(k, carry):
        core_copy(k).wait_send()
        return carry

    lax.fori_loop(0, 2 * Z, finish, 0)

    def finish_y(k, carry):
        y_copy(k).wait_send()
        return carry

    lax.fori_loop(0, Z, finish_y, 0)
    for dz in (1, 2, 3):
        z_copy(dz).wait_send()
    store.wait()


def stats_kernel(own_rows, y_ref, lab_ref, block_ref, dev_ref, cov_ref, owned):
    n = Z * Y * C
    rows = lab_ref.shape[0]
    step = pl.program_id(0)
    me = lax.axis_index("tensor")

    def centre(block):
        part = y_ref[pl.ds(pl.multiple_of(block * rows, rows), rows), :]
        full = part.astype(jnp.float32)
        mean = jnp.sum(full, axis=0, keepdims=True) / rows
        return part, mean, full - mean

    @pl.when(step == 0)
    def _():
        part, mean, dev = centre(me)
        owned[...] = dev.T.astype(jnp.bfloat16)
        lanes = lax.broadcasted_iota(jnp.int32, lab_ref.shape, 1).astype(jnp.float32)
        onehot = jnp.where(lab_ref[...] == lanes, 1.0, 0.0).astype(jnp.bfloat16)
        down = (((0,), (0,)), ((), ()))
        sums = lax.dot_general(onehot, part, down, preferred_element_type=jnp.float32)
        counts = lax.dot_general(
            onehot, jnp.ones_like(part), down, preferred_element_type=jnp.float32
        )
        dev_ref[...] = sums[:CLASSES] / counts[:CLASSES] - mean

    part, _, dev = centre(step)
    gram = jnp.dot(owned[...], dev.astype(jnp.bfloat16), preferred_element_type=jnp.float32)
    cov_ref[...] = (gram / rows).astype(jnp.bfloat16)
    row = lax.broadcasted_iota(jnp.int32, (TILE, rows), 0)
    col = lax.broadcasted_iota(jnp.int32, (TILE, rows), 1)
    pick = jnp.where(col == row + me * own_rows, 1.0, 0.0).astype(jnp.bfloat16)
    taken = jnp.dot(pick, part, preferred_element_type=jnp.float32)
    block_ref[...] = taken[:own_rows].astype(jnp.bfloat16)


def scrub(resid, erase_mean, erase_down, erase_up):
    highest = lax.Precision.HIGHEST
    x = resid.astype(jnp.float32)
    proj = jnp.dot(x - erase_mean, erase_down, precision=highest)
    return (x - jnp.dot(proj, erase_up, precision=highest)).astype(jnp.bfloat16)


def kernel_body(resid, labels, erase_mean, erase_down, erase_up, norm_gain, w_gate, w_up, w_down):
    n = Z * Y * C
    own_rows, depth = resid.shape
    rows, width, units = own_rows * n, depth // n, w_gate.shape[1]
    quarters = TILE // own_rows
    cols = depth // quarters
    scrubbed = scrub(resid, erase_mean, erase_down, erase_up)
    stacked = scrubbed.reshape(own_rows, quarters, cols).transpose(1, 0, 2).reshape(TILE, cols)
    tags = jnp.tile(jnp.broadcast_to(labels, (own_rows, LANES)), (quarters, 1))
    block = jnp.concatenate([stacked, tags.astype(jnp.bfloat16)], axis=1)

    chunks = 8
    bf16, f32 = jnp.bfloat16, jnp.float32
    vmem, hbm = pl.BlockSpec(memory_space=pltpu.VMEM), pl.BlockSpec(memory_space=pl.ANY)
    dma = pltpu.SemaphoreType.DMA
    weights = 3 * depth * units
    gathered, tagged = pl.pallas_call(
        functools.partial(mlp_kernel, own_rows),
        out_shape=(
            jax.ShapeDtypeStruct((n * rows, width), bf16),
            jax.ShapeDtypeStruct((rows, LANES), f32),
        ),
        in_specs=[vmem, vmem, hbm, hbm, hbm],
        out_specs=(hbm, vmem),
        scratch_shapes=[
            pltpu.VMEM((n * TILE, cols + LANES), bf16),
            pltpu.VMEM((rows, depth), bf16),
            pltpu.VMEM((rows, depth), bf16),
            pltpu.VMEM((depth, units), bf16),
            pltpu.VMEM((depth, units), bf16),
            pltpu.VMEM((n, units, width), bf16),
            pltpu.VMEM((rows, units), f32),
            pltpu.VMEM((rows, units), f32),
            pltpu.VMEM((rows, units), bf16),
            pltpu.VMEM((2 * Z, rows, width), bf16),
            pltpu.VMEM((2 * Z, rows, width), bf16),
            pltpu.VMEM((Z, rows, width), bf16),
            pltpu.VMEM((Z, rows, width), bf16),
            pltpu.VMEM((Z - 1, rows, width), bf16),
            pltpu.VMEM((Z - 1, rows, width), bf16),
            pltpu.VMEM((n * rows, width), bf16),
            dma((chunks,)),
            dma((chunks,)),
            dma((n,)),
            dma((n,)),
            dma((n,)),
            dma((n,)),
            dma((n,)),
            dma((2 * Z,)),
            dma((2 * Z,)),
            dma((Z,)),
            dma((Z,)),
            dma((Z - 1,)),
            dma((Z - 1,)),
            dma,
        ],
        compiler_params=pltpu.CompilerParams(
            collective_id=0, has_side_effects=True, vmem_limit_bytes=58 * MIB
        ),
        cost_estimate=pl.CostEstimate(
            flops=2 * rows * weights, bytes_accessed=2 * weights, transcendentals=rows * units
        ),
    )(block, norm_gain.reshape(1, depth), w_gate, w_up, w_down)

    return pl.pallas_call(
        functools.partial(stats_kernel, own_rows),
        grid=(n,),
        out_shape=(
            jax.ShapeDtypeStruct((own_rows, depth), bf16),
            jax.ShapeDtypeStruct((CLASSES, width), f32),
            jax.ShapeDtypeStruct((width, depth), bf16),
        ),
        in_specs=[vmem, vmem],
        out_specs=(
            pl.BlockSpec((own_rows, width), lambda j: (0, j)),
            pl.BlockSpec((CLASSES, width), lambda j: (0, 0)),
            pl.BlockSpec((width, width), lambda j: (0, j)),
        ),
        scratch_shapes=[pltpu.VMEM((width, rows), bf16)],
        compiler_params=pltpu.CompilerParams(vmem_limit_bytes=24 * MIB),
        cost_estimate=pl.CostEstimate(
            flops=2 * rows * width * depth, bytes_accessed=2 * width * depth, transcendentals=0
        ),
    )(gathered, tagged)


def plain_body(resid, labels, erase_mean, erase_down, erase_up, norm_gain, w_gate, w_up, w_down):
    ranks = lax.axis_size("tensor")
    own = lax.axis_index("tensor")
    total_rows = resid.shape[0] * ranks
    width = resid.shape[1] // ranks
    xs = scrub(resid, erase_mean, erase_down, erase_up).astype(jnp.float32)
    normed = (xs * lax.rsqrt(jnp.mean(xs * xs, axis=1, keepdims=True) + EPS) * norm_gain).astype(
        jnp.bfloat16
    )
    piece = lax.all_gather(normed, "tensor", axis=0, tiled=True)
    gate = jnp.dot(piece, w_gate, preferred_element_type=jnp.float32)
    up = jnp.dot(piece, w_up, preferred_element_type=jnp.float32)
    hidden = (jax.nn.silu(gate) * up).astype(jnp.bfloat16)
    summed = lax.psum_scatter(
        jnp.dot(hidden, w_down, preferred_element_type=jnp.float32),
        "tensor",
        scatter_dimension=0,
        tiled=True,
    )
    block_out = (xs + summed).astype(jnp.bfloat16)
    yf = block_out.astype(jnp.float32)
    onehot = (labels == jnp.arange(CLASSES, dtype=jnp.int32)[None, :]).astype(jnp.float32)
    class_sums, counts = lax.psum(
        (jnp.dot(onehot.T, yf, precision=lax.Precision.HIGHEST), jnp.sum(onehot, axis=0)), "tensor"
    )
    mean = jnp.sum(class_sums, axis=0) / total_rows
    deviation = class_sums / counts[:, None] - mean
    class_dev = lax.dynamic_slice_in_dim(deviation, own * width, width, 1)
    centred = (yf - mean).astype(jnp.bfloat16)
    piece = lax.all_gather(centred, "tensor", axis=0, tiled=True)
    owned = lax.dynamic_slice_in_dim(piece, own * width, width, 1)
    gram = lax.dot_general(
        owned, piece, (((0,), (0,)), ((), ())), preferred_element_type=jnp.float32
    )
    return block_out, class_dev, (gram / total_rows).astype(jnp.bfloat16)


def solution(mesh):
    body = kernel_body if mesh.shape["tensor"] == Z * Y * C else plain_body
    return jax.shard_map(
        body,
        mesh=mesh,
        in_specs=(
            P(("groups", "tensor"), None),
            P(("groups", "tensor"), None),
            P(),
            P(),
            P(),
            P(),
            P(None, "tensor"),
            P(None, "tensor"),
            P("tensor", None),
        ),
        out_specs=(
            P(("groups", "tensor"), None),
            P("groups", "tensor"),
            P(("groups", "tensor"), None),
        ),
        check_vma=False,
    )
```

time: 322 us -> 76.9 us (0.24)
  waiting for transfers between devices: 238 us -> 0 us
  Pallas kernels: 0 us -> 69.5 us
  matrix products: 33.3 us -> 2.87 us
  blocking collectives: 24.4 us -> 0 us
  between operations: 14.5 us -> 0.67 us
  other arithmetic: 5.66 us -> 1.34 us
    unnamed x5 -> x0, waiting for transfers between devices: 94.7 us -> none
    psum x1 -> x0, waiting for transfers between devices: 91.2 us -> none  [body(): lax.psum((jnp.dot(onehot.T, yf, precision=highest), jnp.sum(onehot, axis=...]
    pallas_call x0 -> x2, Pallas kernels: none -> 69.5 us  [the longest x1 60.2 us: kernel_body(): pl.pallas_call(functools.partial(mlp_kernel, own_rows), out_shape=(jax.Sh...]
    all_gather x2 -> x0, waiting for transfers between devices: 52.3 us -> none  [the longest x1 38.6 us: body(): piece = lax.all_gather(normed, 'tensor', axis=0, tiled=True)]
    dot_general x6 -> x2, matrix products: 33.3 us -> 2.87 us  [the longest x1 1.66 us: scrub(): proj = jnp.dot(x - erase_mean, erase_down, precision=highest)]
    psum x1 -> x0, blocking collectives: 24.4 us -> none  [body(): lax.psum((jnp.dot(onehot.T, yf, precision=highest), jnp.sum(onehot, axis=...]
  transfers between devices with their start and end apart: 4 -> 0, of which waited for: 4 -> 0; matrix products, arithmetic and copies ran while one was open for 1% -> 0% of each run, Pallas kernels for 0% -> 0%
where the time goes in v1:
time: 76.9 us; the launch traced here: 76.5 us
  Pallas kernels  69.5 us (90%)
  matrix products  2.87 us (4%)
  local copies, waits for them, and re-layouts  2.17 us (3%)
  other arithmetic  1.34 us (2%)
    pallas_call x1, Pallas kernels, kernel_body(): pl.pallas_call(functools.partial(mlp_kernel, own_rows), out_shape=(jax.Sh...  60.2 us
    pallas_call x1, Pallas kernels, kernel_body(): pl.pallas_call(functools.partial(stats_kernel, own_rows), grid=(n,), out_...  9.26 us
    unnamed x6, local copies, waits for them, and re-layouts  1.98 us
    dot_general x1, matrix products, scrub(): proj = jnp.dot(x - erase_mean, erase_down, precision=highest)  1.66 us

profile of v1, /device:TPU:11, one launch (start us, length us, event | category | flops | bytes accessed | tf_op | source)
XLA Modules:
  0.0 76.5 jit_solution(11202161517669360469)
XLA Ops:
  0.6 0.0 copy-start
  0.6 0.7 convert_bitcast_fusion
  1.4 0.1 convert_element_type.21
  1.4 1.7 %fusion.1 = f32[4,8]{1,0:T(4,128)S(1)} fusion(f32[8192,8]{0,1:T(8,128)} %param.12, bf16[4,8192]{1,0:T(4,128)(2,1)} %param.9, f32[8192]{0:T(1024)} %param.11), kind=kOutput, calls=%fused_computation.3 | convolution fusion | flops 3211264 | bytes 360576 | tf_op jit(solution)/shard_map/dot_general | solution.py:325
  3.1 0.1 tile.10
  3.2 0.0 copy-done
  3.2 1.2 %fusion = bf16[4,8192]{1,0:T(4,128)(2,1)S(1)} fusion(f32[4,8]{1,0:T(4,128)S(1)} %fusion.1, f32[8,8192]{1,0:T(8,128)S(1)} %copy-done, bf16[4,8192]{1,0:T(4,128)(2,1)} %param.9), kind=kOutput, calls=%fused_computation.1 | convolution fusion | flops 3244032 | bytes 393344 | tf_op jit(solution)/shard_map/dot_general | solution.py:326
  4.4 0.6 pad_maximum_fusion.block_ref
  5.1 60.2 %shard_map.112 = (bf16[1024,512]{1,0:T(8,128)(2,1)}, f32[64,128]{1,0:T(8,128)}) custom-call(bf16[16,2176]{1,0:T(8,128)(2,1)} %pad_maximum_fusion.block_ref, f32[1,8192]{1,0:T(1,128)} %bitcast.10, bf16[8192,896]{1,0:T(8,128)(2,1)} %wg_hbm.1, bf16[8192,896]{1,0:T(8,128)(2,1)} %wu_hbm.1, bf16[896,8192]{1,0:T(8,128)(2,1)} %wd_hbm.1), custom_call_target="tpu_custom_call" | custom-call | flops 2818572288 | bytes 44040192 | tf_op jit(solution)/shard_map/pallas_call | solution.py:345
  65.3 0.0 copy-start.1
  65.3 1.2 %copy-done.1 = bf16[1024,512]{1,0:T(8,128)(2,1)S(1)} copy-done((bf16[1024,512]{1,0:T(8,128)(2,1)S(1)}, bf16[1024,512]{1,0:T(8,128)(2,1)}, u32[]{:S(2)}) %copy-start.1) | copy-done | bytes 1048600
  66.5 0.0 copy-start.2
  66.5 0.8 copy-done.2
  67.3 9.3 %shard_map.113 = (bf16[4,8192]{1,0:T(4,128)(2,1)}, f32[8,512]{1,0:T(8,128)}, bf16[512,8192]{1,0:T(8,128)(2,1)}) custom-call(bf16[1024,512]{1,0:T(8,128)(2,1)S(1)} %copy-done.1, f32[64,128]{1,0:T(8,128)S(1)} %copy-done.2), custom_call_target="tpu_custom_call" | custom-call | flops 536870912 | bytes 8388608 | tf_op jit(solution)/shard_map/pallas_call | solution.py:393
  (2 shorter events, 0.0 us)
Async XLA Ops:
  0.6 2.5 %copy-start = (f32[8,8192]{1,0:T(8,128)S(1)}, f32[8,8192]{1,0:T(8,128)}, u32[]{:S(2)}) copy-start(f32[8,8192]{1,0:T(8,128)} %param.13) | copy-start | bytes 786436
  65.3 1.2 %copy-start.1 = (bf16[1024,512]{1,0:T(8,128)(2,1)S(1)}, bf16[1024,512]{1,0:T(8,128)(2,1)}, u32[]{:S(2)}) copy-start(bf16[1024,512]{1,0:T(8,128)(2,1)} %get-tuple-element.5.y_ref) | copy-start | bytes 3145732
  66.5 0.8 copy-start.2

commit v2 on v1

--- a/solution.py
+++ b/solution.py
@@ -12,6 +12,7 @@
 TILE = 16
 LANES = 128
 MIB = 1 << 20
+GROUP = 2
 Z, Y, C = 4, 2, 2
 
 
@@ -26,6 +27,11 @@
 
 def at_rows(ref, block, rows):
     return ref.at[pl.ds(pl.multiple_of(block * rows, rows), rows)]
+
+
+def far_first(z):
+    low = z < Z // 2
+    return [jnp.where(low, 3, 0), jnp.where(low, 2, 1), jnp.where(low, 1 - z, 5 - z)]
 
 
 def remote(src, dst, send, recv, peer):
@@ -55,34 +61,41 @@
         part = at_rows(buf, block, rows)
         remote(part, part, send.at[0], recv.at[block], peer).wait_recv()
 
-    for dz in (2, 1, 3):
-        push(me, index_of((z + dz) % Z, y, c))
+    others = far_first(z)
+    for to in others:
+        push(me, index_of(to, y, c))
     push(me, across)
     push(me, sibling)
-    for dz in (1, 3, 2):
-        block = index_of((z + dz) % Z, y, c)
+    for to in others:
+        block = index_of(to, y, c)
         await_block(block, block)
         push(block, across)
         push(block, sibling)
-    for dz in (0, 1, 3, 2):
-        block = index_of((z + dz) % Z, 1 - y, c)
+    for to in [z] + others:
+        block = index_of(to, 1 - y, c)
         await_block(block, across)
         push(block, sibling)
-    for dz in (0, 1, 3, 2):
-        for to in (y, 1 - y):
-            await_block(index_of((z + dz) % Z, to, 1 - c), sibling)
+    for to in range(Z):
+        for line in (y, 1 - y):
+            await_block(index_of(to, line, 1 - c), sibling)
     return started
 
 
 def mlp_kernel(
     own_rows,
-    block_ref,
+    resid_ref,
+    labels_ref,
+    mean_ref,
+    down_ref,
+    up_ref,
     gain_ref,
     wg_hbm,
     wu_hbm,
     wd_hbm,
     y_hbm,
+    own_ref,
     lab_ref,
+    stack,
     xg,
     xs,
     xn,
@@ -137,13 +150,19 @@
         part = pl.ds(pl.multiple_of(block * width, width), width)
         return pltpu.make_async_copy(wd_hbm.at[:, part], wd.at[pos], d_sem.at[pos])
 
-    order = (
-        [index_of(k, 1 - y, 1 - c) for k in range(Z)]
-        + [index_of(k, y, 1 - c) for k in range(Z)]
-        + [index_of(k, 1 - y, c) for k in range(Z)]
-        + [index_of((z + dz) % Z, y, c) for dz in (2, 1, 3)]
-        + [me]
-    )
+    turns = far_first(z) + [z]
+
+    def turn(k):
+        low = z < Z // 2
+        third = jnp.where(low, 1 - z, 5 - z)
+        two = jnp.where(low, 3 - k, k)
+        return jnp.where(k == 3, z, jnp.where(k == 2, third, two))
+
+    order = [
+        index_of(to, line, core)
+        for line, core in ((1 - y, 1 - c), (y, 1 - c), (1 - y, c), (y, c))
+        for to in turns
+    ]
 
     barrier = pltpu.get_barrier_semaphore()
     peers = [index_of((z + dz) % Z, y, c) for dz in (1, 2, 3)] + [across, sibling]
@@ -156,8 +175,19 @@
         load_up(k).start()
     for pos in range(n):
         load_down(pos, order[pos]).start()
-    own_part = pl.ds(pl.multiple_of(me * TILE, TILE), TILE)
-    xg[own_part, :] = block_ref[...]
+
+    x = resid_ref[...].astype(jnp.float32)
+    from_mean = x - mean_ref[...]
+    erased = jnp.zeros_like(x)
+    for i in range(CLASSES):
+        proj = jnp.sum(from_mean * down_ref[i : i + 1, :], axis=1, keepdims=True)
+        erased = erased + proj * up_ref[i : i + 1, :]
+    scrubbed = x - erased
+    tags = jnp.broadcast_to(labels_ref[...].astype(jnp.float32), (own_rows, LANES))
+    for q in range(quarters):
+        stack[q * own_rows : (q + 1) * own_rows, :cols] = scrubbed[:, q * cols : (q + 1) * cols]
+        stack[q * own_rows : (q + 1) * own_rows, cols:] = tags
+    xg[pl.ds(pl.multiple_of(me * TILE, TILE), TILE), :] = stack[...].astype(jnp.bfloat16)
     pl.semaphore_wait(barrier, len(peers))
 
     started = all_gather(xg, TILE, ag1_send, ag1_recv)
@@ -219,17 +249,14 @@
     def y_copy(k):
         return remote(s_y.at[k], r_y.at[k], y_send.at[k], y_recv.at[k], across)
 
-    def z_copy(dz):
+    def z_copy(to):
+        slot = (to - z + Z) % Z - 1
         return remote(
-            s_z.at[dz - 1],
-            r_z.at[dz - 1],
-            z_send.at[dz - 1],
-            z_recv.at[dz - 1],
-            index_of((z + dz) % Z, y, c),
+            s_z.at[slot], r_z.at[slot], z_send.at[slot], z_recv.at[slot], index_of(to, y, c)
         )
 
     def to_core(k, carry):
-        block = index_of(k % Z, jnp.where(k < Z, 1 - y, y), 1 - c)
+        block = index_of(turn(k % Z), jnp.where(k < Z, 1 - y, y), 1 - c)
         s_core[k] = share(k, block).astype(jnp.bfloat16)
         core_copy(k).start()
         return carry
@@ -237,7 +264,7 @@
     lax.fori_loop(0, 2 * Z, to_core, 0)
 
     def to_y(k, carry):
-        mine = share(2 * Z + k, index_of(k, 1 - y, c))
+        mine = share(2 * Z + k, index_of(turn(k), 1 - y, c))
         core_copy(k).wait_recv()
         s_y[k] = (mine + r_core[k].astype(jnp.float32)).astype(jnp.bfloat16)
         y_copy(k).start()
@@ -245,22 +272,23 @@
 
     lax.fori_loop(0, Z, to_y, 0)
 
-    def chip_rows(pos, to):
-        mine = share(pos, index_of(to, y, c))
-        core_copy(Z + to).wait_recv()
-        y_copy(to).wait_recv()
-        return mine + r_core[Z + to].astype(jnp.float32) + r_y[to].astype(jnp.float32)
-
-    for i, dz in enumerate((2, 1, 3)):
-        s_z[dz - 1] = chip_rows(3 * Z + i, (z + dz) % Z).astype(jnp.bfloat16)
-        z_copy(dz).start()
-    summed = chip_rows(n - 1, z)
-    for dz in (1, 3, 2):
-        z_copy(dz).wait_recv()
+    def chip_rows(k):
+        mine = share(3 * Z + k, index_of(turns[k], y, c))
+        core_copy(Z + k).wait_recv()
+        y_copy(k).wait_recv()
+        return mine + r_core[Z + k].astype(jnp.float32) + r_y[k].astype(jnp.float32)
+
+    for k in range(Z - 1):
+        s_z[(turns[k] - z + Z) % Z - 1] = chip_rows(k).astype(jnp.bfloat16)
+        z_copy(turns[k]).start()
+    summed = chip_rows(Z - 1)
+    for dz in range(1, Z):
+        z_copy((z + dz) % Z).wait_recv()
         summed = summed + r_z[dz - 1].astype(jnp.float32)
     mine = pl.ds(pl.multiple_of(me * width, width), width)
     kept = (xs[:, mine].astype(jnp.float32) + summed).astype(jnp.bfloat16)
     out[pl.ds(pl.multiple_of(me * rows, rows), rows), :] = kept
+    own_ref[...] = kept
 
     started += all_gather(out, rows, ag2_send, ag2_recv)
     store = pltpu.make_async_copy(out, y_hbm, o_sem)
@@ -279,26 +307,24 @@
         return carry
 
     lax.fori_loop(0, Z, finish_y, 0)
-    for dz in (1, 2, 3):
-        z_copy(dz).wait_send()
+    for dz in range(1, Z):
+        z_copy((z + dz) % Z).wait_send()
     store.wait()
 
 
-def stats_kernel(own_rows, y_ref, lab_ref, block_ref, dev_ref, cov_ref, owned):
-    n = Z * Y * C
-    rows = lab_ref.shape[0]
-    step = pl.program_id(0)
+def stats_kernel(own_rows, y_ref, own_ref, lab_ref, block_ref, dev_ref, cov_ref, owned):
+    rows, width = own_ref.shape
     me = lax.axis_index("tensor")
 
-    def centre(block):
-        part = y_ref[pl.ds(pl.multiple_of(block * rows, rows), rows), :]
+    def centre(part):
         full = part.astype(jnp.float32)
-        mean = jnp.sum(full, axis=0, keepdims=True) / rows
-        return part, mean, full - mean
-
-    @pl.when(step == 0)
+        mean = jnp.sum(full, axis=0, keepdims=True) * (1.0 / rows)
+        return mean, full - mean
+
+    @pl.when(pl.program_id(0) == 0)
     def _():
-        part, mean, dev = centre(me)
+        part = own_ref[...]
+        mean, dev = centre(part)
         owned[...] = dev.T.astype(jnp.bfloat16)
         lanes = lax.broadcasted_iota(jnp.int32, lab_ref.shape, 1).astype(jnp.float32)
         onehot = jnp.where(lab_ref[...] == lanes, 1.0, 0.0).astype(jnp.bfloat16)
@@ -309,14 +335,17 @@
         )
         dev_ref[...] = sums[:CLASSES] / counts[:CLASSES] - mean
 
-    part, _, dev = centre(step)
-    gram = jnp.dot(owned[...], dev.astype(jnp.bfloat16), preferred_element_type=jnp.float32)
-    cov_ref[...] = (gram / rows).astype(jnp.bfloat16)
     row = lax.broadcasted_iota(jnp.int32, (TILE, rows), 0)
     col = lax.broadcasted_iota(jnp.int32, (TILE, rows), 1)
     pick = jnp.where(col == row + me * own_rows, 1.0, 0.0).astype(jnp.bfloat16)
-    taken = jnp.dot(pick, part, preferred_element_type=jnp.float32)
-    block_ref[...] = taken[:own_rows].astype(jnp.bfloat16)
+    for i in range(GROUP):
+        at = slice(i * width, (i + 1) * width)
+        part = y_ref[i * rows : (i + 1) * rows, :]
+        _, dev = centre(part)
+        gram = jnp.dot(owned[...], dev.astype(jnp.bfloat16), preferred_element_type=jnp.float32)
+        cov_ref[:, at] = (gram * (1.0 / rows)).astype(jnp.bfloat16)
+        taken = jnp.dot(pick, part, preferred_element_type=jnp.float32)
+        block_ref[:, at] = taken[:own_rows].astype(jnp.bfloat16)
 
 
 def scrub(resid, erase_mean, erase_down, erase_up):
@@ -332,25 +361,22 @@
     rows, width, units = own_rows * n, depth // n, w_gate.shape[1]
     quarters = TILE // own_rows
     cols = depth // quarters
-    scrubbed = scrub(resid, erase_mean, erase_down, erase_up)
-    stacked = scrubbed.reshape(own_rows, quarters, cols).transpose(1, 0, 2).reshape(TILE, cols)
-    tags = jnp.tile(jnp.broadcast_to(labels, (own_rows, LANES)), (quarters, 1))
-    block = jnp.concatenate([stacked, tags.astype(jnp.bfloat16)], axis=1)
-
     chunks = 8
     bf16, f32 = jnp.bfloat16, jnp.float32
     vmem, hbm = pl.BlockSpec(memory_space=pltpu.VMEM), pl.BlockSpec(memory_space=pl.ANY)
     dma = pltpu.SemaphoreType.DMA
     weights = 3 * depth * units
-    gathered, tagged = pl.pallas_call(
+    gathered, owned, tagged = pl.pallas_call(
         functools.partial(mlp_kernel, own_rows),
         out_shape=(
             jax.ShapeDtypeStruct((n * rows, width), bf16),
+            jax.ShapeDtypeStruct((rows, width), bf16),
             jax.ShapeDtypeStruct((rows, LANES), f32),
         ),
-        in_specs=[vmem, vmem, hbm, hbm, hbm],
-        out_specs=(hbm, vmem),
+        in_specs=[vmem] * 6 + [hbm] * 3,
+        out_specs=(hbm, vmem, vmem),
         scratch_shapes=[
+            pltpu.VMEM((TILE, cols + LANES), f32),
             pltpu.VMEM((n * TILE, cols + LANES), bf16),
             pltpu.VMEM((rows, depth), bf16),
             pltpu.VMEM((rows, depth), bf16),
@@ -388,28 +414,42 @@
         cost_estimate=pl.CostEstimate(
             flops=2 * rows * weights, bytes_accessed=2 * weights, transcendentals=rows * units
         ),
-    )(block, norm_gain.reshape(1, depth), w_gate, w_up, w_down)
+    )(
+        resid,
+        labels,
+        erase_mean.reshape(1, depth),
+        erase_down.T,
+        erase_up,
+        norm_gain.reshape(1, depth),
+        w_gate,
+        w_up,
+        w_down,
+    )
 
     return pl.pallas_call(
         functools.partial(stats_kernel, own_rows),
-        grid=(n,),
+        grid=(n // GROUP,),
         out_shape=(
             jax.ShapeDtypeStruct((own_rows, depth), bf16),
             jax.ShapeDtypeStruct((CLASSES, width), f32),
             jax.ShapeDtypeStruct((width, depth), bf16),
         ),
-        in_specs=[vmem, vmem],
+        in_specs=[
+            pl.BlockSpec((GROUP * rows, width), lambda j: (j, 0)),
+            pl.BlockSpec((rows, width), lambda j: (0, 0)),
+            pl.BlockSpec((rows, LANES), lambda j: (0, 0)),
+        ],
         out_specs=(
-            pl.BlockSpec((own_rows, width), lambda j: (0, j)),
+            pl.BlockSpec((own_rows, GROUP * width), lambda j: (0, j)),
             pl.BlockSpec((CLASSES, width), lambda j: (0, 0)),
-            pl.BlockSpec((width, width), lambda j: (0, j)),
+            pl.BlockSpec((width, GROUP * width), lambda j: (0, j)),
         ),
         scratch_shapes=[pltpu.VMEM((width, rows), bf16)],
         compiler_params=pltpu.CompilerParams(vmem_limit_bytes=24 * MIB),
         cost_estimate=pl.CostEstimate(
             flops=2 * rows * width * depth, bytes_accessed=2 * width * depth, transcendentals=0
         ),
-    )(gathered, tagged)
+    )(gathered, owned, tagged)
 
 
 def plain_body(resid, labels, erase_mean, erase_down, erase_up, norm_gain, w_gate, w_up, w_down):

time: 76.9 us -> 67.1 us (0.87)
  Pallas kernels: 69.5 us -> 61.8 us
  matrix products: 2.87 us -> 0 us
  local copies, waits for them, and re-layouts: 2.17 us -> 4.13 us
  other arithmetic: 1.34 us -> 0 us
    pallas_call x1, Pallas kernels: 60.2 us -> 55.4 us  [kernel_body(): pl.pallas_call(functools.partial(mlp_kernel, own_rows), out_shape=(jax.Sh...]
    pallas_call x1, Pallas kernels: 9.26 us -> 6.36 us  [kernel_body(): pl.pallas_call(functools.partial(stats_kernel, own_rows), grid=(n // GROU...]
    dot_general x2 -> x0, matrix products: 2.87 us -> none  [the longest x1 1.66 us: scrub(): proj = jnp.dot(x - erase_mean, erase_down, precision=highest)]
    unnamed x6 -> x7, local copies, waits for them, and re-layouts: 1.98 us -> 4.13 us
where the time goes in v2:
time: 67.1 us; the launch traced here: 66.6 us
  Pallas kernels  61.8 us (92%)
  local copies, waits for them, and re-layouts  4.13 us (6%)
    pallas_call x1, Pallas kernels, kernel_body(): pl.pallas_call(functools.partial(mlp_kernel, own_rows), out_shape=(jax.Sh...  55.4 us
    pallas_call x1, Pallas kernels, kernel_body(): pl.pallas_call(functools.partial(stats_kernel, own_rows), grid=(n // GROU...  6.36 us
    unnamed x7, local copies, waits for them, and re-layouts  4.13 us

profile of v2, /device:TPU:11, one launch (start us, length us, event | category | flops | bytes accessed | tf_op | source)
XLA Modules:
  0.0 66.6 jit_solution(3970734328393045602)
XLA Ops:
  0.6 1.3 %copy.12.labels_ref = s32[4,1]{1,0:T(4,128)} copy(s32[4,1]{0,1:T(1,128)} %param.10) | data formatting | bytes 32 | tf_op args[1]
  1.9 55.4 %shard_map.112 = (bf16[1024,512]{1,0:T(8,128)(2,1)}, bf16[64,512]{1,0:T(8,128)(2,1)}, f32[64,128]{1,0:T(8,128)}) custom-call(bf16[4,8192]{1,0:T(4,128)(2,1)} %resid_ref.1, s32[4,1]{1,0:T(4,128)} %copy.12.labels_ref, f32[1,8192]{1,0:T(1,128)} %bitcast.4, f32[8,8192]{1,0:T(8,128)} %bitcast.3, f32[8,8192]{1,0:T(8,128)} %up_ref.1, f32[1,8192]{1,0:T(1,128)} %bitcast.5, ...), custom_call_target="tpu_custom_call" | custom-call | flops 2818572288 | bytes 44040192 | tf_op jit(solution)/shard_map/pallas_call | solution.py:369
  57.4 0.0 copy-start
  57.4 1.2 %copy-done = bf16[1024,512]{1,0:T(8,128)(2,1)S(1)} copy-done((bf16[1024,512]{1,0:T(8,128)(2,1)S(1)}, bf16[1024,512]{1,0:T(8,128)(2,1)}, u32[]{:S(2)}) %copy-start) | copy-done | bytes 1048600
  58.6 0.0 copy-start.1
  58.6 0.8 %copy-done.1 = bf16[64,512]{1,0:T(8,128)(2,1)S(1)} copy-done((bf16[64,512]{1,0:T(8,128)(2,1)S(1)}, bf16[64,512]{1,0:T(8,128)(2,1)}, u32[]{:S(2)}) %copy-start.1) | copy-done | bytes 65560
  59.4 0.0 copy-start.2
  59.4 0.8 %copy-done.2 = f32[64,128]{1,0:T(8,128)S(1)} copy-done((f32[64,128]{1,0:T(8,128)S(1)}, f32[64,128]{1,0:T(8,128)}, u32[]{:S(2)}) %copy-start.2) | copy-done | bytes 32792
  60.2 6.4 %shard_map.113 = (bf16[4,8192]{1,0:T(4,128)(2,1)}, f32[8,512]{1,0:T(8,128)}, bf16[512,8192]{1,0:T(8,128)(2,1)}) custom-call(bf16[1024,512]{1,0:T(8,128)(2,1)S(1)} %copy-done, bf16[64,512]{1,0:T(8,128)(2,1)S(1)} %copy-done.1, f32[64,128]{1,0:T(8,128)S(1)} %copy-done.2), custom_call_target="tpu_custom_call" | custom-call | flops 536870912 | bytes 8388608 | tf_op jit(solution)/shard_map/pallas_call | solution.py:429
Async XLA Ops:
  57.4 1.2 %copy-start = (bf16[1024,512]{1,0:T(8,128)(2,1)S(1)}, bf16[1024,512]{1,0:T(8,128)(2,1)}, u32[]{:S(2)}) copy-start(bf16[1024,512]{1,0:T(8,128)(2,1)} %get-tuple-element.6.y_ref) | copy-start | bytes 3145732
  58.6 0.8 %copy-start.1 = (bf16[64,512]{1,0:T(8,128)(2,1)S(1)}, bf16[64,512]{1,0:T(8,128)(2,1)}, u32[]{:S(2)}) copy-start(bf16[64,512]{1,0:T(8,128)(2,1)} %get-tuple-element.7.own_ref) | copy-start | bytes 196612
  59.4 0.8 %copy-start.2 = (f32[64,128]{1,0:T(8,128)S(1)}, f32[64,128]{1,0:T(8,128)}, u32[]{:S(2)}) copy-start(f32[64,128]{1,0:T(8,128)} %get-tuple-element.8.lab_ref) | copy-start | bytes 98308

commit v3 on v2

--- a/solution.py
+++ b/solution.py
@@ -12,7 +12,7 @@
 TILE = 16
 LANES = 128
 MIB = 1 << 20
-GROUP = 2
+GROUP = 4
 Z, Y, C = 4, 2, 2
 
 
@@ -183,7 +183,11 @@
         proj = jnp.sum(from_mean * down_ref[i : i + 1, :], axis=1, keepdims=True)
         erased = erased + proj * up_ref[i : i + 1, :]
     scrubbed = x - erased
-    tags = jnp.broadcast_to(labels_ref[...].astype(jnp.float32), (own_rows, LANES))
+    down = lax.broadcasted_iota(jnp.int32, (own_rows, own_rows), 0)
+    right = lax.broadcasted_iota(jnp.int32, (own_rows, own_rows), 1)
+    label_row = jnp.broadcast_to(labels_ref[...].astype(jnp.float32), (own_rows, own_rows))
+    label_column = jnp.sum(jnp.where(down == right, label_row, 0.0), axis=1, keepdims=True)
+    tags = jnp.broadcast_to(label_column, (own_rows, LANES))
     for q in range(quarters):
         stack[q * own_rows : (q + 1) * own_rows, :cols] = scrubbed[:, q * cols : (q + 1) * cols]
         stack[q * own_rows : (q + 1) * own_rows, cols:] = tags
@@ -416,7 +420,7 @@
         ),
     )(
         resid,
-        labels,
+        labels.T,
         erase_mean.reshape(1, depth),
         erase_down.T,
         erase_up,
@@ -445,7 +449,7 @@
             pl.BlockSpec((width, GROUP * width), lambda j: (0, j)),
         ),
         scratch_shapes=[pltpu.VMEM((width, rows), bf16)],
-        compiler_params=pltpu.CompilerParams(vmem_limit_bytes=24 * MIB),
+        compiler_params=pltpu.CompilerParams(vmem_limit_bytes=58 * MIB),
         cost_estimate=pl.CostEstimate(
             flops=2 * rows * width * depth, bytes_accessed=2 * width * depth, transcendentals=0
         ),

time: 67.1 us -> 63 us (0.939)
  local copies, waits for them, and re-layouts: 4.13 us -> 0 us
    unnamed x7 -> x0, local copies, waits for them, and re-layouts: 4.13 us -> none
where the time goes in v3:
time: 63 us; the launch traced here: 62.6 us
  Pallas kernels  61.9 us (98%)
  between operations  0.64 us (1%)
    pallas_call x1, Pallas kernels, kernel_body(): pl.pallas_call(functools.partial(mlp_kernel, own_rows), out_shape=(jax.Sh...  55.5 us
    pallas_call x1, Pallas kernels, kernel_body(): pl.pallas_call(functools.partial(stats_kernel, own_rows), grid=(n // GROU...  6.47 us

profile of v3, /device:TPU:11, one launch (start us, length us, event | category | flops | bytes accessed | tf_op | source)
XLA Modules:
  0.0 62.6 jit_solution(10244501827135898050)
XLA Ops:
  0.6 55.5 %shard_map.112 = (bf16[1024,512]{1,0:T(8,128)(2,1)}, bf16[64,512]{1,0:T(8,128)(2,1)}, f32[64,128]{1,0:T(8,128)}) custom-call(bf16[4,8192]{1,0:T(4,128)(2,1)} %resid_ref.1, s32[1,4]{1,0:T(1,128)} %bitcast.7, f32[1,8192]{1,0:T(1,128)} %bitcast.5, f32[8,8192]{1,0:T(8,128)} %bitcast.4, f32[8,8192]{1,0:T(8,128)} %up_ref.1, f32[1,8192]{1,0:T(1,128)} %bitcast.6, ...), custom_call_target="tpu_custom_call" | custom-call | flops 2818572288 | bytes 44040192 | tf_op jit(solution)/shard_map/pallas_call | solution.py:373
  56.1 6.5 %shard_map.113 = (bf16[4,8192]{1,0:T(4,128)(2,1)}, f32[8,512]{1,0:T(8,128)}, bf16[512,8192]{1,0:T(8,128)(2,1)}) custom-call(bf16[1024,512]{1,0:T(8,128)(2,1)} %get-tuple-element.6.y_ref, bf16[64,512]{1,0:T(8,128)(2,1)} %get-tuple-element.7.own_ref, f32[64,128]{1,0:T(8,128)} %get-tuple-element.8.lab_ref), custom_call_target="tpu_custom_call" | custom-call | flops 536870912 | bytes 8388608 | tf_op jit(solution)/shard_map/pallas_call | solution.py:433

commit v4 on v3

--- a/solution.py
+++ b/solution.py
@@ -62,9 +62,9 @@
         remote(part, part, send.at[0], recv.at[block], peer).wait_recv()
 
     others = far_first(z)
+    push(me, across)
     for to in others:
         push(me, index_of(to, y, c))
-    push(me, across)
     push(me, sibling)
     for to in others:
         block = index_of(to, y, c)

time: 63 us -> 63 us (level)
  no operation moved by 1% of the time
where the time goes in v4:
time: 63 us; the launch traced here: 62.6 us
  Pallas kernels  62 us (98%)
  between operations  0.64 us (1%)
    pallas_call x1, Pallas kernels, kernel_body(): pl.pallas_call(functools.partial(mlp_kernel, own_rows), out_shape=(jax.Sh...  55.5 us
    pallas_call x1, Pallas kernels, kernel_body(): pl.pallas_call(functools.partial(stats_kernel, own_rows), grid=(n // GROU...  6.47 us

profile of v4, /device:TPU:11, one launch (start us, length us, event | category | flops | bytes accessed | tf_op | source)
XLA Modules:
  0.0 62.6 jit_solution(7452277738151519474)
XLA Ops:
  0.6 55.5 %shard_map.112 = (bf16[1024,512]{1,0:T(8,128)(2,1)}, bf16[64,512]{1,0:T(8,128)(2,1)}, f32[64,128]{1,0:T(8,128)}) custom-call(bf16[4,8192]{1,0:T(4,128)(2,1)} %resid_ref.1, s32[1,4]{1,0:T(1,128)} %bitcast.7, f32[1,8192]{1,0:T(1,128)} %bitcast.5, f32[8,8192]{1,0:T(8,128)} %bitcast.4, f32[8,8192]{1,0:T(8,128)} %up_ref.1, f32[1,8192]{1,0:T(1,128)} %bitcast.6, ...), custom_call_target="tpu_custom_call" | custom-call | flops 2818572288 | bytes 44040192 | tf_op jit(solution)/shard_map/pallas_call | solution.py:373
  56.1 6.5 %shard_map.113 = (bf16[4,8192]{1,0:T(4,128)(2,1)}, f32[8,512]{1,0:T(8,128)}, bf16[512,8192]{1,0:T(8,128)(2,1)}) custom-call(bf16[1024,512]{1,0:T(8,128)(2,1)} %get-tuple-element.6.y_ref, bf16[64,512]{1,0:T(8,128)(2,1)} %get-tuple-element.7.own_ref, f32[64,128]{1,0:T(8,128)} %get-tuple-element.8.lab_ref), custom_call_target="tpu_custom_call" | custom-call | flops 536870912 | bytes 8388608 | tf_op jit(solution)/shard_map/pallas_call | solution.py:433
